TPU v7x, 128 devices: a whole 4x4x4 slice. The times are simulated.
128 devices in a mesh: tm: 32 (over y_lo, z, x), freq: 4 (over y_hi, core).
Axes of the slice: x: 4, y: 4 (y_hi: 2, y_lo: 2; y = y_hi * 2 + y_lo), z: 4, core: 2. Of those that a mesh axis runs over, the one named last changes fastest.
Arguments:
- waveform: float32 [4194304], P(('tm', 'freq')), may hold values from -24.5 to 24.5
- starts: int32 [16384], P(('tm', 'freq')), may hold values from 0 to 4194303, as said below
- templates: float32 [1024, 512], P('freq'), may hold values from 0.05 to 2
- activations: float32 [16384, 512], P('tm', 'freq'), may hold values from 0.05 to 2
Outputs:
- templates_out: float32 [1024, 512], P('freq')
- activations_out: float32 [16384, 512], P('tm', 'freq')
Inputs may be any that keep to these rules, and one draw needn't show every extreme that they name: Frame j starts within the stretch of 32768 samples numbered j // 128: (j // 128) * 32768 <= starts[j] < (j // 128 + 1) * 32768.
All inputs are finite; a program needn't handle non-finite values.
Results may differ from a plain program's by a relative error of at most 0.003.
The roundings to bfloat16 on the way count: a program that leaves them out, or rounds other values in their place, can miss the bound.
Values may be sent and summed in bfloat16 or wider, within the bound.
A program may use at most 64 MiB of HBM per device.

v0:
```python
import math

import jax
import jax.numpy as jnp
from jax import lax
from jax.sharding import PartitionSpec as P

FLEN = 2048
BINS = 1024
ITERS = 2


def from_behind(block, axis, distance):
    devices = range(lax.axis_size(axis))
    route = [(i - distance, i) for i in devices if i - distance in devices]
    return lax.ppermute(block, axis, route)


def fourier_table(length, bins):
    row_index = jnp.arange(length, dtype=jnp.int32)[:, None]
    bin_index = jnp.arange(bins, dtype=jnp.int32)[None, :]
    phase = (row_index * bin_index % length).astype(jnp.float32) * (2.0 * math.pi / length)
    return jnp.concatenate([jnp.cos(phase), -jnp.sin(phase)], axis=1).astype(jnp.bfloat16)


def hann_window(length):
    steps_all = jnp.arange(length, dtype=jnp.int32).astype(jnp.float32)
    return 0.5 - 0.5 * jnp.cos(steps_all * (2.0 * math.pi / length))


def rebuild_ratios(energy, acts_half, templates_half):
    rebuilt = lax.dot_general(
        acts_half, templates_half, (((1,), (1,)), ((), ())), preferred_element_type=jnp.float32
    )
    return (energy / rebuilt).astype(jnp.bfloat16)


def shards(waveform, starts, templates, activations):
    next_rim = from_behind(waveform[:FLEN], ("tm", "freq"), -1)
    extended = jnp.concatenate([waveform, next_rim])
    local_starts = starts % waveform.shape[0]
    window = hann_window(FLEN)
    frames = jax.vmap(lambda offset: lax.dynamic_slice(extended, (offset,), (FLEN,)))(local_starts)
    frames = (frames * window[None, :]).astype(jnp.bfloat16)
    spectrum = jnp.dot(frames, fourier_table(FLEN, BINS), preferred_element_type=jnp.float32)
    energy = (spectrum[:, :BINS] ** 2 + spectrum[:, BINS:] ** 2) * 0.25
    acts_now = lax.all_to_all(activations, "freq", split_axis=0, concat_axis=1, tiled=True)
    weights_now = lax.all_gather(templates, "freq", axis=0, tiled=True)
    for iteration in range(ITERS):
        templates_half = weights_now.astype(jnp.bfloat16)
        acts_half = acts_now.astype(jnp.bfloat16)
        ratios = rebuild_ratios(energy, acts_half, templates_half)
        numerator = jnp.dot(ratios, templates_half, preferred_element_type=jnp.float32)
        template_mass = jnp.sum(weights_now, axis=0)
        acts_now = acts_now * numerator / template_mass[None, :]
        acts_half = acts_now.astype(jnp.bfloat16)
        ratios = rebuild_ratios(energy, acts_half, templates_half)
        template_numerator = lax.dot_general(
            ratios, acts_half, (((0,), (0,)), ((), ())), preferred_element_type=jnp.float32
        )
        column_totals = jnp.sum(acts_half, axis=0, dtype=jnp.float32)
        template_numerator, column_totals = lax.psum(
            (template_numerator, column_totals), ("tm", "freq")
        )
        weights_now = weights_now * template_numerator / column_totals[None, :]
    own_bins = templates.shape[0]
    templates_out = lax.dynamic_slice_in_dim(
        weights_now, lax.axis_index("freq") * own_bins, own_bins, 0
    )
    activations_out = lax.all_to_all(acts_now, "freq", split_axis=1, concat_axis=0, tiled=True)
    return (templates_out, activations_out)


def solution(mesh):
    in_specs = (P(("tm", "freq")), P(("tm", "freq")), P("freq", None), P("tm", "freq"))
    out_specs = (P("freq", None), P("tm", "freq"))
    return jax.shard_map(shards, mesh=mesh, in_specs=in_specs, out_specs=out_specs, check_vma=False)
```

profile of v0, /device:TPU:1, one launch (start us, length us, event | category | flops | bytes accessed | tf_op | source)
XLA Modules:
  0.0 575.8 jit_solution(10659771763737941033)
XLA Ops:
  8.6 3.3 collective-permute-start
  11.9 4.7 all-to-all-start
  17.3 34.9 %negate_convert_fusion = (bf16[2048,1024]{1,0:T(8,128)(2,1)}, bf16[2048,1024]{1,0:T(8,128)(2,1)}) fusion(), kind=kLoop, calls=%fused_computation.11 | loop fusion | flops 35651584 | bytes 8388608 | tf_op jit(solution)/shard_map/convert.1
  52.3 191.3 %while.1 = (s32[]{:T(128)}, f32[34816]{0:T(1024)S(1)}, s32[128,1]{0,1:T(1,128)S(1)}, f32[128,2048]{1,0:T(8,128)S(1)}, s32[]{:T(128)}, /*index=5*/s32[]{:T(128)}) while((s32[]{:T(128)}, f32[34816]{0:T(1024)S(1)}, s32[128,1]{0,1:T(1,128)S(1)}, f32[128,2048]{1,0:T(8,128)S(1)}, s32[]{:T(128)}, /*index=5*/s32[]{:T(128)}) %tuple.24), condition=%wide.while_cond, body=%wide.while_body.sunk | while | flops 2 | bytes 32857 | solution.py:43
  54.4 0.7 dynamic-slice.7
  57.4 0.7 dynamic-slice.7
  60.4 0.7 dynamic-slice.7
  63.4 0.7 dynamic-slice.7
  66.4 0.7 dynamic-slice.7
  69.3 0.7 dynamic-slice.7
  70.8 0.7 dynamic-slice.7
  72.3 0.7 dynamic-slice.7
  73.8 0.7 dynamic-slice.7
  76.8 0.7 dynamic-slice.7
  79.8 0.7 dynamic-slice.7
  82.8 0.7 dynamic-slice.7
  85.8 0.7 dynamic-slice.7
  88.8 0.7 dynamic-slice.7
  91.8 0.7 dynamic-slice.7
  94.7 0.7 dynamic-slice.7
  97.7 0.7 dynamic-slice.7
  99.2 0.7 dynamic-slice.7
  100.7 0.7 dynamic-slice.7
  102.2 0.7 dynamic-slice.7
  105.2 0.7 dynamic-slice.7
  108.2 0.7 dynamic-slice.7
  111.2 0.7 dynamic-slice.7
  114.2 0.7 dynamic-slice.7
  117.2 0.7 dynamic-slice.7
  120.1 0.7 dynamic-slice.7
  123.1 0.7 dynamic-slice.7
  126.1 0.7 dynamic-slice.7
  127.6 0.7 dynamic-slice.7
  129.1 0.7 dynamic-slice.7
  130.6 0.7 dynamic-slice.7
  133.6 0.7 dynamic-slice.7
  136.6 0.7 dynamic-slice.7
  139.6 0.7 dynamic-slice.7
  142.6 0.7 dynamic-slice.7
  145.5 0.7 dynamic-slice.7
  148.5 0.7 dynamic-slice.7
  151.5 0.7 dynamic-slice.7
  154.5 0.7 dynamic-slice.7
  156.0 0.7 dynamic-slice.7
  157.5 0.7 dynamic-slice.7
  159.0 0.7 dynamic-slice.7
  162.0 0.7 dynamic-slice.7
  165.0 0.7 dynamic-slice.7
  168.0 0.7 dynamic-slice.7
  170.9 0.7 dynamic-slice.7
  173.9 0.7 dynamic-slice.7
  243.6 4.3 fusion.3
  248.0 1.9 reduce_sum.36
  249.9 3.0 convert_reduce_fusion.1
  252.9 2.1 fusion.21
  255.1 71.4 %psum.29 = f32[512]{0:T(512)S(1)} all-reduce(f32[512]{0:T(512)S(1)} %get-tuple-element.20), channel_id=1, replica_groups=mesh['tm'=32,'freq'=4] {'tm','freq'}, use_global_device_ids=true, to_apply=%region_3.4 | all-reduce | flops 512 | bytes 4096 | tf_op jit(solution)/shard_map/psum | solution.py:62
  326.5 82.8 %all-reduce.3.cloned.1.call-done = f32[1024,512]{1,0:T(8,128)} async-done(((f32[1024,512]{1,0:T(8,128)}), f32[1024,512]{1,0:T(8,128)}) %all-reduce.3.cloned.1.call-update) | async-done | bytes 2097168 | tf_op jit(solution)/shard_map/psum | solution.py:62
  409.3 3.2 fusion.45
  412.5 3.0 convert_reduce_fusion
  415.6 2.1 fusion.20
  418.4 5.0 all-to-all-start.1
  423.4 65.3 %psum.31 = f32[512]{0:T(512)S(1)} all-reduce(f32[512]{0:T(512)S(1)} %get-tuple-element.22), channel_id=1, replica_groups=mesh['tm'=32,'freq'=4] {'tm','freq'}, use_global_device_ids=true, to_apply=%region_7.8 | all-reduce | flops 512 | bytes 4096 | tf_op jit(solution)/shard_map/psum | solution.py:62
  488.7 77.9 %all-reduce.5.cloned.1.call-done = f32[1024,512]{1,0:T(8,128)} async-done(((f32[1024,512]{1,0:T(8,128)}), f32[1024,512]{1,0:T(8,128)}) %all-reduce.5.cloned.1.call-update) | async-done | bytes 2097168 | tf_op jit(solution)/shard_map/psum | solution.py:62
  566.6 1.9 fusion.22
  (361 shorter events, 158.0 us)
Async XLA Ops:
  7.2 240.8 %all-gather.2.cloned.1.call-start = ((), (), s32[]{:S(2)}) async-start(), calls=%async_computation.2 | async-start | bytes 2621440 | tf_op jit(solution)/shard_map/all_gather | solution.py:48
  8.6 43.7 %collective-permute-start = (f32[2048]{0:T(1024)S(1)}, f32[2048]{0:T(1024)S(1)}, u32[]{:S(2)}, u32[]{:S(2)}) collective-permute-start(f32[2048]{0:T(1024)S(1)} %slice.9), channel_id=1, source_target_pairs={{1,0},{2,1},{3,2},{4,3},{5,4},{6,5},{7,6},{8,7},{9,8},{10,9},{11,1... | collective-permute-start | bytes 24584 | tf_op jit(solution)/shard_map/ppermute | solution.py:16
  11.9 238.0 %all-to-all-start = ((f32[4,128,128]{2,1,0:T(8,128)}), f32[4,128,128]{2,1,0:T(8,128)S(1)}, u32[]{:S(2)}, u32[]{:S(2)}) async-start(f32[4,128,128]{2,1,0:T(8,128)} %bitcast.33), calls=%async_computation | async-start | bytes 524288 | tf_op jit(solution)/shard_map/all_to_all | solution.py:47
  16.6 392.7 %all-reduce.3.cloned.1.call-start = ((), (), s32[]{:S(2)}) async-start(), calls=%async_computation.3 | async-start | bytes 4194304 | tf_op jit(solution)/shard_map/psum | solution.py:62
  17.3 35.0 %copy-start.2 = (f32[32768]{0:T(1024)S(1)}, f32[32768]{0:T(1024)}, u32[]{:S(2)}) copy-start(f32[32768]{0:T(1024)} %param.4) | copy-start | bytes 393220
  248.0 4.9 copy-start
  255.0 311.6 %all-reduce.5.cloned.1.call-start = ((), (), s32[]{:S(2)}) async-start(), calls=%async_computation.4 | async-start | bytes 4194304 | tf_op jit(solution)/shard_map/psum | solution.py:62
  412.5 3.1 copy-start.1
  418.4 70.3 %all-to-all-start.1 = ((f32[128,4,128]{2,0,1:T(8,128)}), f32[128,4,128]{2,0,1:T(8,128)S(1)}, u32[]{:S(2)}, u32[]{:S(2)}) async-start(f32[128,4,128]{2,0,1:T(8,128)} %copy_bitcast_fusion), calls=%async_computation.1 | async-start | bytes 524288 | tf_op jit(solution)/shard_map/all_to_all | solution.py:70
Sparse Core Ops, SparseCore 0:
  9.7 30.3 all-gather.1
  255.2 154.0 all-reduce.2
  417.8 148.7 all-reduce.4
where the time goes:
time: 578 us; the launch traced here: 576 us
  local copies, waits for them, and re-layouts  190 us (33%)
  waiting for transfers between devices  161 us (28%)
  blocking collectives  137 us (24%)
  other arithmetic  42.8 us (7%)
  matrix products  14.5 us (3%)
  between operations  13.8 us (2%)
  starting transfers between devices  13 us (2%)
    gather x384, local copies, waits for them, and re-layouts  188 us
    psum x2, waiting for transfers between devices, shards(): lax.psum((template_numerator, column_totals), ('tm', 'freq'))  161 us
    psum x2, blocking collectives, shards(): lax.psum((template_numerator, column_totals), ('tm', 'freq'))  137 us
    another operation x1, other arithmetic  34.9 us
  transfers between devices with their start and end apart: 6, of which 2 were waited for; matrix products, arithmetic and copies ran while one was open for 40% of the time, Pallas kernels for 0%

commit v1 on v0

v1 whole, which is shorter than its diff:
```python
import jax
import jax.numpy as jnp
import numpy as np
from jax import lax
from jax.experimental import pallas as pl
from jax.experimental.pallas import tpu as pltpu
from jax.sharding import PartitionSpec as P

FLEN = 2048
BINS = 1024
K = 512
ITERS = 2
SEG = 32768
FR = 128
GROUPS = 4
MESH = pl.DeviceIdType.MESH
F32 = jnp.float32
BF16 = jnp.bfloat16


def half_tables():
    row = np.arange(FLEN, dtype=np.int64)[:, None]
    tables = []
    for core in range(2):
        bins = np.concatenate([np.arange(256) + 256 * core, np.arange(256) + 512 + 256 * core])
        phase = ((row * bins[None, :]) % FLEN).astype(np.float32) * np.float32(2.0 * np.pi / FLEN)
        tables.append(np.concatenate([np.cos(phase), -np.sin(phase)], axis=1))
    return np.stack(tables).astype(jnp.bfloat16)


def hann_window():
    steps = np.arange(FLEN, dtype=np.float32) * np.float32(2.0 * np.pi / FLEN)
    return (np.float32(0.5) - np.float32(0.5) * np.cos(steps)).reshape(16, 128)


def hops(offset):
    return sum(min(v, 4 - v) for v in offset)


OFFSETS = sorted(
    [(dx, dy, dz) for dz in range(4) for dy in range(4) for dx in range(4) if dx or dy or dz],
    key=lambda offset: -hops(offset),
)


def dot(a, b, dims):
    return lax.dot_general(a, b, (dims, ((), ())), preferred_element_type=F32)


def kernel(
    wave_hbm, starts, window, table_hbm, templ_hbm, act_hbm, w_out, a_out,
    wave, table, templ, acts, gathered, frames, energy, energy_t, wb, own_w, w_last,
    part, part_got, t_send, t_got, tot, tot_got, mass, mass_half,
    local_sem, rim_sem, frame_send, frame_recv, act_send, act_recv, w_send, w_recv,
    part_send, part_recv, t_sems, mass_send, mass_recv, fin_sem, y_sem, z_sem,
):
    tm = lax.axis_index("tm")
    fr = lax.axis_index("freq")
    x, z, y_lo = lax.rem(tm, 4), lax.rem(lax.div(tm, 4), 4), lax.div(tm, 16)
    y_hi, core = lax.div(fr, 2), lax.rem(fr, 2)
    y = 2 * y_hi + y_lo
    xs = [lax.rem(x + d, 4) for d in range(4)]
    zs = [lax.rem(z + d, 4) for d in range(4)]
    ys = [lax.rem(y + d, 4) for d in range(4)]
    y_los = [lax.rem(v, 2) for v in ys]
    y_his = [lax.div(v, 2) for v in ys]

    def chip(dx, dy, dz):
        return (y_los[dy] * 16 + zs[dz] * 4 + xs[dx], y_his[dy] * 2 + core)

    def remote(src, dst, send, recv, device):
        return pltpu.make_async_remote_copy(
            src_ref=src, dst_ref=dst, send_sem=send, recv_sem=recv,
            device_id=device, device_id_type=MESH,
        )

    sibling = (tm, 2 * y_hi + 1 - core)
    across = (tm, 2 * (1 - y_hi) + core)
    beside = (lax.rem(tm + 16, 32), 2 * (1 - y_hi) + core)
    place = 4 * tm + fr
    following = lax.rem(place + 1, 128)
    previous = lax.rem(place + 127, 128)
    following = (lax.div(following, 4), lax.rem(following, 4))
    previous = (lax.div(previous, 4), lax.rem(previous, 4))

    copies = [
        pltpu.make_async_copy(wave_hbm, wave.at[pl.ds(0, 256)], local_sem.at[0]),
        pltpu.make_async_copy(act_hbm, acts.at[fr], local_sem.at[1]),
        pltpu.make_async_copy(templ_hbm, templ, local_sem.at[2]),
        pltpu.make_async_copy(table_hbm.at[core], table, local_sem.at[3]),
    ]
    barrier = pltpu.get_barrier_semaphore()
    axis_peers = [chip(d, 0, 0) for d in (1, 2, 3)]
    y_peers = [chip(0, d, 0) for d in (1, 2, 3)]
    z_peers = [chip(0, 0, d) for d in (1, 2, 3)]
    for device in [following, sibling] + axis_peers + y_peers + z_peers:
        pl.semaphore_signal(barrier, inc=1, device_id=device, device_id_type=MESH)
    for copy in copies:
        copy.start()
    copies[2].wait()
    for h in range(2):
        wb[h, pl.ds(16 * y_hi, 16)] = templ[:, 256 * h : 256 * h + 256].astype(BF16).reshape(16, 16, 256)
    mass[0, pl.ds(y_hi, 1)] = jnp.sum(templ[...], axis=0, keepdims=True).reshape(1, 1, K)
    g = 16 * y_hi + 4 * z + x
    for h in range(2):

        @pl.when(y_lo == h)
        def _():
            own_w[...] = templ[pl.ds(pl.multiple_of(16 * (4 * z + x), 16), 16), 256 * h : 256 * h + 256]

    copies[0].wait()
    copies[1].wait()
    pl.semaphore_wait(barrier, 11)

    rim = remote(wave.at[pl.ds(0, 16)], wave.at[pl.ds(256, 16)], rim_sem.at[0], rim_sem.at[1], previous)
    rim.start()
    here = pl.ds(pl.multiple_of(256 * y_hi, 256), 256)
    there = pl.ds(pl.multiple_of(256 * (1 - y_hi), 256), 256)
    act_across = remote(acts.at[fr, there], acts.at[fr, there], act_send.at[0], act_recv.at[0], across)
    act_across.start()
    act_sibling = remote(acts.at[fr, here], acts.at[fr, here], act_send.at[1], act_recv.at[1], sibling)
    act_sibling.start()
    w_copies = []
    for h in range(2):
        rows = wb.at[h, pl.ds(16 * y_hi, 16)]
        w_copies.append(remote(rows, rows, w_send.at[h], w_recv.at[h], beside))
    w_copies.append(remote(mass.at[0, y_hi], mass.at[0, y_hi], w_send.at[2], w_recv.at[2], beside))
    for copy in w_copies:
        copy.start()
    for device in y_peers:
        pl.semaphore_signal(y_sem, inc=1, device_id=device, device_id_type=MESH)

    rim.wait()

    @pl.when(place == 127)
    def _():
        wave[pl.ds(256, 16)] = jnp.zeros((16, 128), F32)

    lanes = lax.broadcasted_iota(jnp.int32, (16, 128), 1)
    scale = window[...]
    size = FR // GROUPS
    frame_copies = []
    for group in range(GROUPS):

        def gather(i, carry):
            start = lax.rem(starts[group * size + i], SEG)
            row, shift = lax.div(start, 128), lax.rem(start, 128)
            low = wave[pl.ds(row, 16), :]
            high = wave[pl.ds(row + 1, 16), :]
            joined = jnp.where(lanes >= shift, low, high)
            rolled = pltpu.roll(joined, lax.rem(128 - shift, 128), 1)
            gathered[pl.ds(i, 16, stride=size), :] = rolled * scale
            return carry

        lax.fori_loop(0, size, gather, 0, unroll=8)
        rows = pl.ds(pl.multiple_of(FR * core + group * size, size), size)
        for i in range(16):
            frames[rows, 128 * i : 128 * i + 128] = gathered[size * i : size * i + size, :].astype(BF16)
        copy = remote(frames.at[rows], frames.at[rows], frame_send.at[group], frame_recv.at[group], sibling)
        copy.start()
        frame_copies.append(copy)

    act_across.wait()
    far = 2 * (1 - y_hi) + core
    act_pass = remote(acts.at[far, here], acts.at[far, here], act_send.at[2], act_recv.at[2], sibling)
    act_pass.start()
    pl.semaphore_wait(y_sem, 3)
    for device in z_peers:
        pl.semaphore_signal(z_sem, inc=1, device_id=device, device_id_type=MESH)
    copies[3].wait()
    for copy in frame_copies:
        copy.wait()
    for j in range(2):
        cos = dot(frames[...], table[:, 256 * j : 256 * j + 256], ((1,), (0,)))
        sin = dot(frames[...], table[:, 512 + 256 * j : 768 + 256 * j], ((1,), (0,)))
        square = (cos * cos + sin * sin) * 0.25
        energy[:, 256 * j : 256 * j + 256] = square
        energy_t[256 * j : 256 * j + 256, :] = square.T
    for copy in w_copies:
        copy.wait()
    act_sibling.wait()
    act_pass.wait()
    pl.semaphore_wait(z_sem, 3)

    for t in range(ITERS):
        w_half = [wb[h].reshape(512, 256) for h in range(2)]
        if t == 0:
            half = mass[0, 0] + mass[0, 1]
        else:
            half = jnp.concatenate(
                [jnp.sum(w.astype(F32), axis=0, keepdims=True) for w in w_half], axis=1
            )
        mass_half[t, 0] = half
        mass_copy = remote(mass_half.at[t, 0], mass_half.at[t, 1], mass_send.at[t], mass_recv.at[t], sibling)
        mass_copy.start()
        hb = [acts[f, here].astype(BF16) for f in range(4)]
        hb = [jnp.concatenate(hb[:2], axis=1), jnp.concatenate(hb[2:], axis=1)]
        rebuilt = dot(hb[0], w_half[0], ((1,), (1,))) + dot(hb[1], w_half[1], ((1,), (1,)))
        ratios = (energy[...] / rebuilt).astype(BF16)
        part_copies = []
        for h in range(2):
            part[t, h] = dot(ratios, w_half[h], ((1,), (0,)))
            copy = remote(part.at[t, h], part_got.at[t, h], part_send.at[t, h], part_recv.at[t, h], sibling)
            copy.start()
            part_copies.append(copy)
        mass_copy.wait()
        inverse = 1.0 / (mass_half[t, 0] + mass_half[t, 1])
        hb = []
        for h in range(2):
            part_copies[h].wait()
            factor = (part[t, h] + part_got[t, h]) * inverse[:, 256 * h : 256 * h + 256]
            pieces = []
            for k in range(2):
                new = acts[2 * h + k, here] * factor[:, 128 * k : 128 * k + 128]
                acts[2 * h + k, here] = new
                pieces.append(new.astype(BF16))
            hb.append(jnp.concatenate(pieces, axis=1))
            tot[t, h] = jnp.sum(hb[h].astype(F32), axis=0, keepdims=True)
        if t == ITERS - 1:
            final = remote(acts.at[far, here], acts.at[far, here], fin_sem.at[0], fin_sem.at[1], across)
            final.start()

        rebuilt = dot(w_half[0], hb[0], ((1,), (1,))) + dot(w_half[1], hb[1], ((1,), (1,)))
        ratios = (energy_t[...] / rebuilt).astype(BF16)
        for h in range(2):
            t_send[h] = dot(ratios, hb[h], ((1,), (0,))).astype(BF16).reshape(32, 16, 256)
        for slot, (dx, dy, dz) in enumerate(OFFSETS):
            owner = 16 * y_his[dy] + 4 * zs[dz] + xs[dx]
            remote(
                t_send.at[y_los[dy], owner], t_got.at[slot], t_sems.at[0], t_sems.at[1], chip(dx, dy, dz)
            ).start()
            remote(
                tot.at[t, y_los[dy]], tot_got.at[slot], t_sems.at[2], t_sems.at[3], chip(dx, dy, dz)
            ).start()
        total = tot[t, y_lo]
        summed = t_send[y_lo, g].astype(F32)
        for s in (2, 3):
            pltpu.make_async_copy(tot_got, tot_got, t_sems.at[s]).wait()
        for s in (0, 1):
            pltpu.make_async_copy(t_got, t_got, t_sems.at[s]).wait()
        total = total + jnp.sum(tot_got[...], axis=0)
        summed = summed + jnp.sum(t_got[...].astype(F32), axis=0)
        new_w = own_w[...] * summed / total
        if t < ITERS - 1:
            own_w[...] = new_w
            wb[y_lo, g] = new_w.astype(BF16)
            for dx, dy, dz in OFFSETS:
                remote(
                    wb.at[y_lo, g], wb.at[y_lo, g], t_sems.at[4], t_sems.at[5], chip(dx, dy, dz)
                ).start()
            for s in (4, 5):
                pltpu.make_async_copy(t_got, t_got, t_sems.at[s]).wait()
        else:
            w_last[y_lo, 4 * z + x] = new_w.astype(BF16)
            count = 0
            for dx, dy, dz in OFFSETS:
                if dy > 1:
                    continue
                other = 1 - y_lo if dy else y_lo
                device = (16 * other + 4 * zs[dz] + xs[dx], fr)
                mine = w_last.at[y_lo, 4 * z + x]
                remote(mine, mine, t_sems.at[6], t_sems.at[7], device).start()
                count += 1
            a_out[here, :] = acts[fr, here]
            final.wait()
            a_out[there, :] = acts[fr, there]
            waited = t_got.at[pl.ds(0, count)]
            for s in (6, 7):
                pltpu.make_async_copy(waited, waited, t_sems.at[s]).wait()
            for h in range(2):
                w_out[:, 256 * h : 256 * h + 256] = w_last[h].reshape(256, 256).astype(F32)


def shards(waveform, starts, templates, activations):
    hbm = pl.BlockSpec(memory_space=pl.ANY)
    vmem = pl.BlockSpec(memory_space=pltpu.VMEM)
    dma = pltpu.SemaphoreType.DMA
    scratch = [
        pltpu.VMEM((272, 128), F32),
        pltpu.VMEM((FLEN, 1024), BF16),
        pltpu.VMEM((256, K), F32),
        pltpu.VMEM((4, 512, 128), F32),
        pltpu.VMEM((16 * FR // GROUPS, 128), F32),
        pltpu.VMEM((256, FLEN), BF16),
        pltpu.VMEM((256, 512), F32),
        pltpu.VMEM((512, 256), F32),
        pltpu.VMEM((2, 32, 16, 256), BF16),
        pltpu.VMEM((16, 256), F32),
        pltpu.VMEM((2, 16, 16, 256), BF16),
        pltpu.VMEM((ITERS, 2, 256, 256), F32),
        pltpu.VMEM((ITERS, 2, 256, 256), F32),
        pltpu.VMEM((2, 32, 16, 256), BF16),
        pltpu.VMEM((63, 16, 256), BF16),
        pltpu.VMEM((ITERS, 2, 1, 256), F32),
        pltpu.VMEM((63, 1, 256), F32),
        pltpu.VMEM((1, 2, 1, K), F32),
        pltpu.VMEM((ITERS, 2, 1, K), F32),
        dma((4,)),
        dma((2,)),
        dma((GROUPS,)),
        dma((GROUPS,)),
        dma((3,)),
        dma((3,)),
        dma((3,)),
        dma((3,)),
        dma((ITERS, 2)),
        dma((ITERS, 2)),
        dma((8,)),
        dma((ITERS,)),
        dma((ITERS,)),
        dma((2,)),
        pltpu.SemaphoreType.REGULAR,
        pltpu.SemaphoreType.REGULAR,
    ]
    return pl.pallas_call(
        kernel,
        out_shape=(
            jax.ShapeDtypeStruct((256, K), F32),
            jax.ShapeDtypeStruct((512, 128), F32),
        ),
        in_specs=[hbm, pl.BlockSpec(memory_space=pltpu.SMEM), vmem, hbm, hbm, hbm],
        out_specs=(vmem, vmem),
        scratch_shapes=scratch,
        compiler_params=pltpu.CompilerParams(
            collective_id=0, has_side_effects=True, vmem_limit_bytes=48 * 2**20
        ),
    )(
        waveform.reshape(256, 128),
        starts,
        jnp.asarray(hann_window()),
        jnp.asarray(half_tables()),
        templates,
        activations,
    )


def solution(mesh):
    in_specs = (P(("tm", "freq")), P(("tm", "freq")), P("freq", None), P("tm", "freq"))
    out_specs = (P("freq", None), P("tm", "freq"))
    return jax.shard_map(shards, mesh=mesh, in_specs=in_specs, out_specs=out_specs, check_vma=False)
```

time: 578 us -> 68.7 us (0.12)
  local copies, waits for them, and re-layouts: 190 us -> 5.74 us
  waiting for transfers between devices: 161 us -> 0 us
  blocking collectives: 137 us -> 0 us
  Pallas kernels: 0 us -> 62 us
  other arithmetic: 42.8 us -> 0 us
  matrix products: 14.5 us -> 0 us
  between operations: 13.8 us -> 0.65 us
  starting transfers between devices: 13 us -> 0 us
    gather x384 -> x0, local copies, waits for them, and re-layouts: 188 us -> none
    psum x2 -> x0, waiting for transfers between devices: 161 us -> none  [shards(): lax.psum((template_numerator, column_totals), ('tm', 'freq'))]
    psum x2 -> x0, blocking collectives: 137 us -> none  [shards(): lax.psum((template_numerator, column_totals), ('tm', 'freq'))]
    pallas_call x0 -> x1, Pallas kernels: none -> 62 us  [shards(): pl.pallas_call(kernel, out_shape=(jax.ShapeDtypeStruct((256, K), F32), ja...]
    another operation x1 -> x0, other arithmetic: 34.9 us -> none
    dot_general x5 -> x0, matrix products: 14.5 us -> none  [the longest x2 6 us: shards(): jnp.dot(ratios, templates_half, preferred_element_type=jnp.float32)]
    all_to_all x2 -> x0, starting transfers between devices: 9.64 us -> none  [the longest x1 4.97 us: shards(): lax.all_to_all(acts_now, 'freq', split_axis=1, concat_axis=0, tiled=True)]
  transfers between devices with their start and end apart: 6 -> 0, of which waited for: 2 -> 0; matrix products, arithmetic and copies ran while one was open for 40% -> 0% of each run, Pallas kernels for 0% -> 0%
where the time goes in v1:
time: 68.7 us; the launch traced here: 68.4 us
  Pallas kernels  62 us (90%)
  local copies, waits for them, and re-layouts  5.74 us (8%)
    pallas_call x1, Pallas kernels, shards(): pl.pallas_call(kernel, out_shape=(jax.ShapeDtypeStruct((256, K), F32), ja...  62 us
    unnamed x12, local copies, waits for them, and re-layouts  5.74 us

profile of v1, /device:TPU:1, one launch (start us, length us, event | category | flops | bytes accessed | tf_op | source)
XLA Modules:
  0.0 68.4 jit_solution(17348001527507533027)
XLA Ops:
  0.6 0.0 copy-start
  0.6 1.0 %copy-done = f32[256,512]{1,0:T(8,128)S(1)} copy-done((f32[256,512]{1,0:T(8,128)S(1)}, f32[256,512]{1,0:T(8,128)}, u32[]{:S(2)}) %copy-start) | copy-done | bytes 524312
  1.7 0.0 copy-start.1
  1.7 0.9 %copy-done.1 = f32[512,128]{1,0:T(8,128)S(1)} copy-done((f32[512,128]{1,0:T(8,128)S(1)}, f32[512,128]{1,0:T(8,128)}, u32[]{:S(2)}) %copy-start.1) | copy-done | bytes 262168
  2.6 0.0 copy-start.2
  2.6 0.9 %copy-done.2 = f32[32768]{0:T(1024)S(1)} copy-done((f32[32768]{0:T(1024)S(1)}, f32[32768]{0:T(1024)}, u32[]{:S(2)}) %copy-start.2) | copy-done | bytes 131096
  3.5 0.0 copy-start.3
  3.5 0.7 %copy-done.3 = f32[16,128]{1,0:T(8,128)S(1)} copy-done((f32[16,128]{1,0:T(8,128)S(1)}, f32[16,128]{1,0:T(8,128)}, u32[]{:S(2)}) %copy-start.3) | copy-done | bytes 8216
  4.2 0.0 copy-start.4
  4.2 0.7 copy-done.4
  4.9 62.0 %shard_map.77 = (f32[256,512]{1,0:T(8,128)S(1)}, f32[512,128]{1,0:T(8,128)S(1)}) custom-call(f32[256,128]{1,0:T(8,128)S(1)} %bitcast.1, s32[128]{0:T(128)S(1)} %copy-done.4, f32[16,128]{1,0:T(8,128)S(1)} %copy-done.3, bf16[2,2048,1024]{2,1,0:T(8,128)(2,1)} %constant.5.clone.table_hbm, f32[256,512]{1,0:T(8,128)S(1)} %copy-done, f32[512,128]{1,0:T(8,128)S(1)} %copy-done.1), custom_call_target="tpu_custom_call" | custom-call | tf_op jit(solution)/shard_map/pallas_call | solution.py:315
  66.9 0.8 %copy.10 = f32[256,512]{1,0:T(8,128)} copy(f32[256,512]{1,0:T(8,128)S(1)} %get-tuple-element.4) | data formatting | bytes 1048576
  67.7 0.7 %copy.11 = f32[512,128]{1,0:T(8,128)} copy(f32[512,128]{1,0:T(8,128)S(1)} %get-tuple-element.5) | data formatting | bytes 524288
Async XLA Ops:
  0.6 1.0 %copy-start = (f32[256,512]{1,0:T(8,128)S(1)}, f32[256,512]{1,0:T(8,128)}, u32[]{:S(2)}) copy-start(f32[256,512]{1,0:T(8,128)} %templ_hbm.1) | copy-start | bytes 1572868
  1.7 0.9 %copy-start.1 = (f32[512,128]{1,0:T(8,128)S(1)}, f32[512,128]{1,0:T(8,128)}, u32[]{:S(2)}) copy-start(f32[512,128]{1,0:T(8,128)} %act_hbm.1) | copy-start | bytes 786436
  2.6 0.9 %copy-start.2 = (f32[32768]{0:T(1024)S(1)}, f32[32768]{0:T(1024)}, u32[]{:S(2)}) copy-start(f32[32768]{0:T(1024)} %param.6) | copy-start | bytes 393220
  3.5 0.7 %copy-start.3 = (f32[16,128]{1,0:T(8,128)S(1)}, f32[16,128]{1,0:T(8,128)}, u32[]{:S(2)}) copy-start(f32[16,128]{1,0:T(8,128)} %constant.4.clone.window) | copy-start | bytes 24580
  4.2 0.7 copy-start.4

commit v2 on v1

--- a/solution.py
+++ b/solution.py
@@ -43,16 +43,22 @@
 )
 
 
+PLANE = sorted(
+    [(dx, dy) for dy in range(4) for dx in range(4) if dx or dy],
+    key=lambda offset: -hops(offset),
+)
+
+
 def dot(a, b, dims):
     return lax.dot_general(a, b, (dims, ((), ())), preferred_element_type=F32)
 
 
 def kernel(
-    wave_hbm, starts, window, table_hbm, templ_hbm, act_hbm, w_out, a_out,
-    wave, table, templ, acts, gathered, frames, energy, energy_t, wb, own_w, w_last,
-    part, part_got, t_send, t_got, tot, tot_got, mass, mass_half,
+    wave_hbm, starts_hbm, window_hbm, table_hbm, templ_hbm, act_hbm, w_out, a_out,
+    starts, window, wave, table, templ, acts, gathered, frames, energy, energy_t, wb, own_w, w_last,
+    vb, part, part_got, t_send, t_got, tot, tot_z, z_got, xy_got, mass, mass_half,
     local_sem, rim_sem, frame_send, frame_recv, act_send, act_recv, w_send, w_recv,
-    part_send, part_recv, t_sems, mass_send, mass_recv, fin_sem, y_sem, z_sem,
+    part_send, part_recv, t_sems, z_sems, xy_sems, mass_send, mass_recv, fin_sem, y_sem, z_sem,
 ):
     tm = lax.axis_index("tm")
     fr = lax.axis_index("freq")
@@ -88,6 +94,8 @@
         pltpu.make_async_copy(act_hbm, acts.at[fr], local_sem.at[1]),
         pltpu.make_async_copy(templ_hbm, templ, local_sem.at[2]),
         pltpu.make_async_copy(table_hbm.at[core], table, local_sem.at[3]),
+        pltpu.make_async_copy(starts_hbm, starts, local_sem.at[4]),
+        pltpu.make_async_copy(window_hbm, window, local_sem.at[5]),
     ]
     barrier = pltpu.get_barrier_semaphore()
     axis_peers = [chip(d, 0, 0) for d in (1, 2, 3)]
@@ -98,15 +106,17 @@
     for copy in copies:
         copy.start()
     copies[2].wait()
-    for h in range(2):
-        wb[h, pl.ds(16 * y_hi, 16)] = templ[:, 256 * h : 256 * h + 256].astype(BF16).reshape(16, 16, 256)
+    for h in range(4):
+        wb[h, pl.ds(16 * y_hi, 16)] = templ[:, 128 * h : 128 * h + 128].astype(BF16).reshape(16, 16, 128)
     mass[0, pl.ds(y_hi, 1)] = jnp.sum(templ[...], axis=0, keepdims=True).reshape(1, 1, K)
     g = 16 * y_hi + 4 * z + x
     for h in range(2):
 
         @pl.when(y_lo == h)
         def _():
-            own_w[...] = templ[pl.ds(pl.multiple_of(16 * (4 * z + x), 16), 16), 256 * h : 256 * h + 256]
+            rows = pl.ds(pl.multiple_of(16 * (4 * z + x), 16), 16)
+            for k in range(2):
+                own_w[k] = templ[rows, 256 * k + 128 * h : 256 * k + 128 * h + 128]
 
     copies[0].wait()
     copies[1].wait()
@@ -121,16 +131,18 @@
     act_sibling = remote(acts.at[fr, here], acts.at[fr, here], act_send.at[1], act_recv.at[1], sibling)
     act_sibling.start()
     w_copies = []
-    for h in range(2):
+    for h in range(4):
         rows = wb.at[h, pl.ds(16 * y_hi, 16)]
         w_copies.append(remote(rows, rows, w_send.at[h], w_recv.at[h], beside))
-    w_copies.append(remote(mass.at[0, y_hi], mass.at[0, y_hi], w_send.at[2], w_recv.at[2], beside))
+    w_copies.append(remote(mass.at[0, y_hi], mass.at[0, y_hi], w_send.at[4], w_recv.at[4], beside))
     for copy in w_copies:
         copy.start()
     for device in y_peers:
         pl.semaphore_signal(y_sem, inc=1, device_id=device, device_id_type=MESH)
 
     rim.wait()
+    copies[4].wait()
+    copies[5].wait()
 
     @pl.when(place == 127)
     def _():
@@ -183,13 +195,14 @@
     pl.semaphore_wait(z_sem, 3)
 
     for t in range(ITERS):
-        w_half = [wb[h].reshape(512, 256) for h in range(2)]
+        w_half = [
+            jnp.concatenate([wb[2 * h].reshape(512, 128), wb[2 * h + 1].reshape(512, 128)], axis=1)
+            for h in range(2)
+        ]
         if t == 0:
             half = mass[0, 0] + mass[0, 1]
         else:
-            half = jnp.concatenate(
-                [jnp.sum(w.astype(F32), axis=0, keepdims=True) for w in w_half], axis=1
-            )
+            half = jnp.concatenate(halves, axis=1)
         mass_half[t, 0] = half
         mass_copy = remote(mass_half.at[t, 0], mass_half.at[t, 1], mass_send.at[t], mass_recv.at[t], sibling)
         mass_copy.start()
@@ -215,67 +228,93 @@
                 acts[2 * h + k, here] = new
                 pieces.append(new.astype(BF16))
             hb.append(jnp.concatenate(pieces, axis=1))
-            tot[t, h] = jnp.sum(hb[h].astype(F32), axis=0, keepdims=True)
+            tot[t, :, 256 * h : 256 * h + 256] = jnp.sum(hb[h].astype(F32), axis=0, keepdims=True)
         if t == ITERS - 1:
             final = remote(acts.at[far, here], acts.at[far, here], fin_sem.at[0], fin_sem.at[1], across)
             final.start()
 
+        for slot in range(3):
+            remote(tot.at[t], z_got.at[t, slot], z_sems.at[0, t], z_sems.at[1, t], z_peers[slot]).start()
+
         rebuilt = dot(w_half[0], hb[0], ((1,), (1,))) + dot(w_half[1], hb[1], ((1,), (1,)))
         ratios = (energy_t[...] / rebuilt).astype(BF16)
         for h in range(2):
-            t_send[h] = dot(ratios, hb[h], ((1,), (0,))).astype(BF16).reshape(32, 16, 256)
-        for slot, (dx, dy, dz) in enumerate(OFFSETS):
-            owner = 16 * y_his[dy] + 4 * zs[dz] + xs[dx]
+            term = dot(ratios, hb[h], ((1,), (0,))).astype(BF16)
+            for k in range(2):
+                t_send[2 * h + k] = term[:, 128 * k : 128 * k + 128].reshape(32, 16, 128)
+            for slot, (dx, dy, dz) in enumerate(OFFSETS):
+                owner = 16 * y_his[dy] + 4 * zs[dz] + xs[dx]
+                remote(
+                    t_send.at[2 * h + y_los[dy], owner], t_got.at[h, slot],
+                    t_sems.at[0, h], t_sems.at[1, h], chip(dx, dy, dz),
+                ).start()
+        for s in range(2):
+            pltpu.make_async_copy(z_got.at[t], z_got.at[t], z_sems.at[s, t]).wait()
+        plane = tot[t]
+        for slot in range(3):
+            plane = plane + z_got[t, slot]
+        tot_z[t] = plane
+        for slot, (dx, dy) in enumerate(PLANE):
             remote(
-                t_send.at[y_los[dy], owner], t_got.at[slot], t_sems.at[0], t_sems.at[1], chip(dx, dy, dz)
+                tot_z.at[t], xy_got.at[t, slot], xy_sems.at[0, t], xy_sems.at[1, t], chip(dx, dy, 0)
             ).start()
-            remote(
-                tot.at[t, y_los[dy]], tot_got.at[slot], t_sems.at[2], t_sems.at[3], chip(dx, dy, dz)
-            ).start()
-        total = tot[t, y_lo]
-        summed = t_send[y_lo, g].astype(F32)
-        for s in (2, 3):
-            pltpu.make_async_copy(tot_got, tot_got, t_sems.at[s]).wait()
-        for s in (0, 1):
-            pltpu.make_async_copy(t_got, t_got, t_sems.at[s]).wait()
-        total = total + jnp.sum(tot_got[...], axis=0)
-        summed = summed + jnp.sum(t_got[...].astype(F32), axis=0)
-        new_w = own_w[...] * summed / total
+
+        for h in range(2):
+            summed = t_send[2 * h + y_lo, g].astype(F32)
+            for s in range(2):
+                pltpu.make_async_copy(t_got.at[h], t_got.at[h], t_sems.at[s, h]).wait()
+            summed = summed + jnp.sum(t_got[h].astype(F32), axis=0)
+            own_w[h] = own_w[h] * summed
+            if t < ITERS - 1:
+                mine = vb.at[2 * h + y_lo, g]
+                peers = [chip(*offset) for offset in OFFSETS]
+            else:
+                mine = w_last.at[2 * h + y_lo, 4 * z + x]
+                peers = [
+                    (16 * (1 - y_lo if dy else y_lo) + 4 * zs[dz] + xs[dx], fr)
+                    for dx, dy, dz in OFFSETS
+                    if dy < 2
+                ]
+            mine[...] = own_w[h].astype(BF16)
+            for device in peers:
+                remote(mine, mine, t_sems.at[2, h], t_sems.at[3, h], device).start()
+        if t == ITERS - 1:
+            final.wait()
+            a_copy = pltpu.make_async_copy(acts.at[fr], a_out, local_sem.at[1])
+            a_copy.start()
+        for s in range(2):
+            pltpu.make_async_copy(xy_got.at[t], xy_got.at[t], xy_sems.at[s, t]).wait()
+        inv_total = 1.0 / (tot_z[t] + jnp.sum(xy_got[t], axis=0))
         if t < ITERS - 1:
-            own_w[...] = new_w
-            wb[y_lo, g] = new_w.astype(BF16)
-            for dx, dy, dz in OFFSETS:
-                remote(
-                    wb.at[y_lo, g], wb.at[y_lo, g], t_sems.at[4], t_sems.at[5], chip(dx, dy, dz)
-                ).start()
-            for s in (4, 5):
-                pltpu.make_async_copy(t_got, t_got, t_sems.at[s]).wait()
-        else:
-            w_last[y_lo, 4 * z + x] = new_w.astype(BF16)
-            count = 0
-            for dx, dy, dz in OFFSETS:
-                if dy > 1:
-                    continue
-                other = 1 - y_lo if dy else y_lo
-                device = (16 * other + 4 * zs[dz] + xs[dx], fr)
-                mine = w_last.at[y_lo, 4 * z + x]
-                remote(mine, mine, t_sems.at[6], t_sems.at[7], device).start()
-                count += 1
-            a_out[here, :] = acts[fr, here]
-            final.wait()
-            a_out[there, :] = acts[fr, there]
-            waited = t_got.at[pl.ds(0, count)]
-            for s in (6, 7):
-                pltpu.make_async_copy(waited, waited, t_sems.at[s]).wait()
             for h in range(2):
-                w_out[:, 256 * h : 256 * h + 256] = w_last[h].reshape(256, 256).astype(F32)
+                low = inv_total[:, 256 * h : 256 * h + 128]
+                high = inv_total[:, 256 * h + 128 : 256 * h + 256]
+                own_w[h] = own_w[h] * jnp.where(y_lo == 0, low, high)
+        halves = []
+        for h in range(2):
+            arrived = t_got.at[h] if t < ITERS - 1 else t_got.at[h, pl.ds(0, 31)]
+            for s in range(2, 4):
+                pltpu.make_async_copy(arrived, arrived, t_sems.at[s, h]).wait()
+            for q in (2 * h, 2 * h + 1):
+                scale_q = inv_total[:, 128 * q : 128 * q + 128]
+                if t < ITERS - 1:
+                    block = vb[q].reshape(512, 128).astype(F32) * scale_q
+                    halves.append(jnp.sum(block, axis=0, keepdims=True))
+                    wb[q] = block.astype(BF16).reshape(32, 16, 128)
+                else:
+                    block = w_last[q].reshape(256, 128).astype(F32)
+                    w_out[:, 128 * q : 128 * q + 128] = block * scale_q
+        if t == ITERS - 1:
+            a_copy.wait()
 
 
 def shards(waveform, starts, templates, activations):
-    hbm = pl.BlockSpec(memory_space=pl.ANY)
+    hbm = pl.BlockSpec(memory_space=pltpu.HBM)
     vmem = pl.BlockSpec(memory_space=pltpu.VMEM)
     dma = pltpu.SemaphoreType.DMA
     scratch = [
+        pltpu.SMEM((FR,), jnp.int32),
+        pltpu.VMEM((16, 128), F32),
         pltpu.VMEM((272, 128), F32),
         pltpu.VMEM((FLEN, 1024), BF16),
         pltpu.VMEM((256, K), F32),
@@ -284,28 +323,33 @@
         pltpu.VMEM((256, FLEN), BF16),
         pltpu.VMEM((256, 512), F32),
         pltpu.VMEM((512, 256), F32),
-        pltpu.VMEM((2, 32, 16, 256), BF16),
-        pltpu.VMEM((16, 256), F32),
-        pltpu.VMEM((2, 16, 16, 256), BF16),
+        pltpu.VMEM((4, 32, 16, 128), BF16),
+        pltpu.VMEM((2, 16, 128), F32),
+        pltpu.VMEM((4, 16, 16, 128), BF16),
+        pltpu.VMEM((4, 32, 16, 128), BF16),
         pltpu.VMEM((ITERS, 2, 256, 256), F32),
         pltpu.VMEM((ITERS, 2, 256, 256), F32),
-        pltpu.VMEM((2, 32, 16, 256), BF16),
-        pltpu.VMEM((63, 16, 256), BF16),
-        pltpu.VMEM((ITERS, 2, 1, 256), F32),
-        pltpu.VMEM((63, 1, 256), F32),
+        pltpu.VMEM((4, 32, 16, 128), BF16),
+        pltpu.VMEM((2, 63, 16, 128), BF16),
+        pltpu.VMEM((ITERS, 1, K), F32),
+        pltpu.VMEM((ITERS, 1, K), F32),
+        pltpu.VMEM((ITERS, 3, 1, K), F32),
+        pltpu.VMEM((ITERS, 15, 1, K), F32),
         pltpu.VMEM((1, 2, 1, K), F32),
         pltpu.VMEM((ITERS, 2, 1, K), F32),
-        dma((4,)),
+        dma((6,)),
         dma((2,)),
         dma((GROUPS,)),
         dma((GROUPS,)),
         dma((3,)),
         dma((3,)),
-        dma((3,)),
-        dma((3,)),
+        dma((5,)),
+        dma((5,)),
         dma((ITERS, 2)),
         dma((ITERS, 2)),
-        dma((8,)),
+        dma((4, 2)),
+        dma((2, ITERS)),
+        dma((2, ITERS)),
         dma((ITERS,)),
         dma((ITERS,)),
         dma((2,)),
@@ -318,11 +362,11 @@
             jax.ShapeDtypeStruct((256, K), F32),
             jax.ShapeDtypeStruct((512, 128), F32),
         ),
-        in_specs=[hbm, pl.BlockSpec(memory_space=pltpu.SMEM), vmem, hbm, hbm, hbm],
-        out_specs=(vmem, vmem),
+        in_specs=[hbm] * 6,
+        out_specs=(vmem, hbm),
         scratch_shapes=scratch,
         compiler_params=pltpu.CompilerParams(
-            collective_id=0, has_side_effects=True, vmem_limit_bytes=48 * 2**20
+            collective_id=0, has_side_effects=True, vmem_limit_bytes=60 * 2**20
         ),
     )(
         waveform.reshape(256, 128),

time: 68.7 us -> 63.2 us (0.920)
  Pallas kernels: 62 us -> 58.9 us
  local copies, waits for them, and re-layouts: 5.74 us -> 3.54 us
    pallas_call x1, Pallas kernels: 62 us -> 58.9 us  [shards(): pl.pallas_call(kernel, out_shape=(jax.ShapeDtypeStruct((256, K), F32), ja...]
    unnamed x12 -> x2, local copies, waits for them, and re-layouts: 5.74 us -> 3.54 us
where the time goes in v2:
time: 63.2 us; the launch traced here: 63.1 us
  Pallas kernels  58.9 us (93%)
  local copies, waits for them, and re-layouts  3.54 us (6%)
  between operations  0.64 us (1%)
    pallas_call x1, Pallas kernels, shards(): pl.pallas_call(kernel, out_shape=(jax.ShapeDtypeStruct((256, K), F32), ja...  58.9 us
    unnamed x2, local copies, waits for them, and re-layouts  3.54 us

profile of v2, /device:TPU:1, one launch (start us, length us, event | category | flops | bytes accessed | tf_op | source)
XLA Modules:
  0.0 63.1 jit_solution(16746355103703939376)
XLA Ops:
  0.6 58.9 %shard_map.77 = (f32[256,512]{1,0:T(8,128)}, f32[512,128]{1,0:T(8,128)}) custom-call(f32[256,128]{1,0:T(8,128)} %bitcast.1, s32[128]{0:T(128)} %starts_hbm.1, f32[16,128]{1,0:T(8,128)} %constant.4.clone.window_hbm, bf16[2,2048,1024]{2,1,0:T(8,128)(2,1)} %constant.5.clone.table_hbm, f32[256,512]{1,0:T(8,128)} %templ_hbm.1, f32[512,128]{1,0:T(8,128)} %act_hbm.1), custom_call_target="tpu_custom_call" | custom-call | tf_op jit(solution)/shard_map/pallas_call | solution.py:359
  59.5 1.9 %copy.10 = f32[256,512]{1,0:T(8,128)} copy(f32[256,512]{1,0:T(8,128)} %get-tuple-element.4) | data formatting | bytes 1048576
  61.4 1.7 %copy.11 = f32[512,128]{1,0:T(8,128)} copy(f32[512,128]{1,0:T(8,128)} %get-tuple-element.5) | data formatting | bytes 524288

commit v3 on v2

--- a/solution.py
+++ b/solution.py
@@ -229,9 +229,6 @@
                 pieces.append(new.astype(BF16))
             hb.append(jnp.concatenate(pieces, axis=1))
             tot[t, :, 256 * h : 256 * h + 256] = jnp.sum(hb[h].astype(F32), axis=0, keepdims=True)
-        if t == ITERS - 1:
-            final = remote(acts.at[far, here], acts.at[far, here], fin_sem.at[0], fin_sem.at[1], across)
-            final.start()
 
         for slot in range(3):
             remote(tot.at[t], z_got.at[t, slot], z_sems.at[0, t], z_sems.at[1, t], z_peers[slot]).start()
@@ -258,6 +255,10 @@
             remote(
                 tot_z.at[t], xy_got.at[t, slot], xy_sems.at[0, t], xy_sems.at[1, t], chip(dx, dy, 0)
             ).start()
+
+        if t == ITERS - 1:
+            final = remote(acts.at[far, here], acts.at[far, here], fin_sem.at[0], fin_sem.at[1], across)
+            final.start()
 
         for h in range(2):
             summed = t_send[2 * h + y_lo, g].astype(F32)

time: 63.2 us -> 60.2 us (0.953)
  Pallas kernels: 58.9 us -> 55.7 us
    pallas_call x1, Pallas kernels: 58.9 us -> 55.7 us  [shards(): pl.pallas_call(kernel, out_shape=(jax.ShapeDtypeStruct((256, K), F32), ja...]
where the time goes in v3:
time: 60.2 us; the launch traced here: 59.9 us
  Pallas kernels  55.7 us (93%)
  local copies, waits for them, and re-layouts  3.54 us (6%)
  between operations  0.64 us (1%)
    pallas_call x1, Pallas kernels, shards(): pl.pallas_call(kernel, out_shape=(jax.ShapeDtypeStruct((256, K), F32), ja...  55.7 us
    unnamed x2, local copies, waits for them, and re-layouts  3.54 us

profile of v3, /device:TPU:1, one launch (start us, length us, event | category | flops | bytes accessed | tf_op | source)
XLA Modules:
  0.0 59.9 jit_solution(16863562370816062314)
XLA Ops:
  0.6 55.7 %shard_map.77 = (f32[256,512]{1,0:T(8,128)}, f32[512,128]{1,0:T(8,128)}) custom-call(f32[256,128]{1,0:T(8,128)} %bitcast.1, s32[128]{0:T(128)} %starts_hbm.1, f32[16,128]{1,0:T(8,128)} %constant.4.clone.window_hbm, bf16[2,2048,1024]{2,1,0:T(8,128)(2,1)} %constant.5.clone.table_hbm, f32[256,512]{1,0:T(8,128)} %templ_hbm.1, f32[512,128]{1,0:T(8,128)} %act_hbm.1), custom_call_target="tpu_custom_call" | custom-call | tf_op jit(solution)/shard_map/pallas_call | solution.py:360
  56.4 1.9 %copy.10 = f32[256,512]{1,0:T(8,128)} copy(f32[256,512]{1,0:T(8,128)} %get-tuple-element.4) | data formatting | bytes 1048576
  58.2 1.7 %copy.11 = f32[512,128]{1,0:T(8,128)} copy(f32[512,128]{1,0:T(8,128)} %get-tuple-element.5) | data formatting | bytes 524288

commit v4 on v3

--- a/solution.py
+++ b/solution.py
@@ -210,9 +210,10 @@
         hb = [jnp.concatenate(hb[:2], axis=1), jnp.concatenate(hb[2:], axis=1)]
         rebuilt = dot(hb[0], w_half[0], ((1,), (1,))) + dot(hb[1], w_half[1], ((1,), (1,)))
         ratios = (energy[...] / rebuilt).astype(BF16)
-        part_copies = []
-        for h in range(2):
-            part[t, h] = dot(ratios, w_half[h], ((1,), (0,)))
+        part_copies, own_part = [], []
+        for h in range(2):
+            own_part.append(dot(ratios, w_half[h], ((1,), (0,))))
+            part[t, h] = own_part[h].astype(BF16)
             copy = remote(part.at[t, h], part_got.at[t, h], part_send.at[t, h], part_recv.at[t, h], sibling)
             copy.start()
             part_copies.append(copy)
@@ -221,7 +222,7 @@
         hb = []
         for h in range(2):
             part_copies[h].wait()
-            factor = (part[t, h] + part_got[t, h]) * inverse[:, 256 * h : 256 * h + 256]
+            factor = (own_part[h] + part_got[t, h].astype(F32)) * inverse[:, 256 * h : 256 * h + 256]
             pieces = []
             for k in range(2):
                 new = acts[2 * h + k, here] * factor[:, 128 * k : 128 * k + 128]
@@ -328,8 +329,8 @@
         pltpu.VMEM((2, 16, 128), F32),
         pltpu.VMEM((4, 16, 16, 128), BF16),
         pltpu.VMEM((4, 32, 16, 128), BF16),
-        pltpu.VMEM((ITERS, 2, 256, 256), F32),
-        pltpu.VMEM((ITERS, 2, 256, 256), F32),
+        pltpu.VMEM((ITERS, 2, 256, 256), BF16),
+        pltpu.VMEM((ITERS, 2, 256, 256), BF16),
         pltpu.VMEM((4, 32, 16, 128), BF16),
         pltpu.VMEM((2, 63, 16, 128), BF16),
         pltpu.VMEM((ITERS, 1, K), F32),

time: 60.2 us -> 59.4 us (0.987)
  Pallas kernels: 55.7 us -> 55 us
    pallas_call x1, Pallas kernels: 55.7 us -> 55 us  [shards(): pl.pallas_call(kernel, out_shape=(jax.ShapeDtypeStruct((256, K), F32), ja...]
where the time goes in v4:
time: 59.4 us; the launch traced here: 59.2 us
  Pallas kernels  55 us (93%)
  local copies, waits for them, and re-layouts  3.54 us (6%)
  between operations  0.64 us (1%)
    pallas_call x1, Pallas kernels, shards(): pl.pallas_call(kernel, out_shape=(jax.ShapeDtypeStruct((256, K), F32), ja...  55 us
    unnamed x2, local copies, waits for them, and re-layouts  3.54 us

profile of v4, /device:TPU:1, one launch (start us, length us, event | category | flops | bytes accessed | tf_op | source)
XLA Modules:
  0.0 59.2 jit_solution(15236229707818266080)
XLA Ops:
  0.6 55.0 %shard_map.77 = (f32[256,512]{1,0:T(8,128)}, f32[512,128]{1,0:T(8,128)}) custom-call(f32[256,128]{1,0:T(8,128)} %bitcast.1, s32[128]{0:T(128)} %starts_hbm.1, f32[16,128]{1,0:T(8,128)} %constant.4.clone.window_hbm, bf16[2,2048,1024]{2,1,0:T(8,128)(2,1)} %constant.5.clone.table_hbm, f32[256,512]{1,0:T(8,128)} %templ_hbm.1, f32[512,128]{1,0:T(8,128)} %act_hbm.1), custom_call_target="tpu_custom_call" | custom-call | tf_op jit(solution)/shard_map/pallas_call | solution.py:361
  55.6 1.9 %copy.10 = f32[256,512]{1,0:T(8,128)} copy(f32[256,512]{1,0:T(8,128)} %get-tuple-element.4) | data formatting | bytes 1048576
  57.5 1.7 %copy.11 = f32[512,128]{1,0:T(8,128)} copy(f32[512,128]{1,0:T(8,128)} %get-tuple-element.5) | data formatting | bytes 524288

commit v5 on v4

--- a/solution.py
+++ b/solution.py
@@ -246,17 +246,6 @@
                     t_send.at[2 * h + y_los[dy], owner], t_got.at[h, slot],
                     t_sems.at[0, h], t_sems.at[1, h], chip(dx, dy, dz),
                 ).start()
-        for s in range(2):
-            pltpu.make_async_copy(z_got.at[t], z_got.at[t], z_sems.at[s, t]).wait()
-        plane = tot[t]
-        for slot in range(3):
-            plane = plane + z_got[t, slot]
-        tot_z[t] = plane
-        for slot, (dx, dy) in enumerate(PLANE):
-            remote(
-                tot_z.at[t], xy_got.at[t, slot], xy_sems.at[0, t], xy_sems.at[1, t], chip(dx, dy, 0)
-            ).start()
-
         if t == ITERS - 1:
             final = remote(acts.at[far, here], acts.at[far, here], fin_sem.at[0], fin_sem.at[1], across)
             final.start()
@@ -280,6 +269,17 @@
             mine[...] = own_w[h].astype(BF16)
             for device in peers:
                 remote(mine, mine, t_sems.at[2, h], t_sems.at[3, h], device).start()
+            if h == 0:
+                for s in range(2):
+                    pltpu.make_async_copy(z_got.at[t], z_got.at[t], z_sems.at[s, t]).wait()
+                plane = tot[t]
+                for slot in range(3):
+                    plane = plane + z_got[t, slot]
+                tot_z[t] = plane
+                for slot, (dx, dy) in enumerate(PLANE):
+                    remote(
+                        tot_z.at[t], xy_got.at[t, slot], xy_sems.at[0, t], xy_sems.at[1, t], chip(dx, dy, 0)
+                    ).start()
         if t == ITERS - 1:
             final.wait()
             a_copy = pltpu.make_async_copy(acts.at[fr], a_out, local_sem.at[1])

time: 59.4 us -> 59.6 us (level)
  no operation moved by 1% of the time
where the time goes in v5:
time: 59.6 us; the launch traced here: 59.3 us
  Pallas kernels  55.1 us (92%)
  local copies, waits for them, and re-layouts  3.54 us (6%)
  between operations  0.64 us (1%)
    pallas_call x1, Pallas kernels, shards(): pl.pallas_call(kernel, out_shape=(jax.ShapeDtypeStruct((256, K), F32), ja...  55.1 us
    unnamed x2, local copies, waits for them, and re-layouts  3.54 us

profile of v5, /device:TPU:1, one launch (start us, length us, event | category | flops | bytes accessed | tf_op | source)
XLA Modules:
  0.0 59.3 jit_solution(5286632419939990032)
XLA Ops:
  0.6 55.1 %shard_map.77 = (f32[256,512]{1,0:T(8,128)}, f32[512,128]{1,0:T(8,128)}) custom-call(f32[256,128]{1,0:T(8,128)} %bitcast.1, s32[128]{0:T(128)} %starts_hbm.1, f32[16,128]{1,0:T(8,128)} %constant.4.clone.window_hbm, bf16[2,2048,1024]{2,1,0:T(8,128)(2,1)} %constant.5.clone.table_hbm, f32[256,512]{1,0:T(8,128)} %templ_hbm.1, f32[512,128]{1,0:T(8,128)} %act_hbm.1), custom_call_target="tpu_custom_call" | custom-call | tf_op jit(solution)/shard_map/pallas_call | solution.py:361
  55.8 1.9 %copy.10 = f32[256,512]{1,0:T(8,128)} copy(f32[256,512]{1,0:T(8,128)} %get-tuple-element.4) | data formatting | bytes 1048576
  57.7 1.7 %copy.11 = f32[512,128]{1,0:T(8,128)} copy(f32[512,128]{1,0:T(8,128)} %get-tuple-element.5) | data formatting | bytes 524288
